TPU v7x, 32 devices: a whole 2x2x4 slice. The times are simulated.
32 devices in a mesh: sx: 4 (over y, x), sy: 4 (over z), freq: 2 (over core).
Axes of the slice: x: 2, y: 2, z: 4, core: 2. Of those that a mesh axis runs over, the one named last changes fastest.
Arguments:
- update_basis: bfloat16 [4, 512, 32, 1024], P('freq', ('sx', 'sy')), may hold values from -0.1875 to 0.1875
- update_coeff: bfloat16 [4, 512, 32, 128], P('freq', ('sx', 'sy')), may hold values from -6 to 6
- owner: int32 [512, 1], P(('sx', 'sy')), may hold values from 0 to 3; in each aligned block of 32 rows (0 to 31, 32 to 63, ...) at most 16 rows name the same one
- sep_rhs: bfloat16 [4, 4, 4, 1024, 128], P('freq', 'sx', 'sy'), may hold values from -6 to 6
- coupling: float32 [4, 4, 4, 4, 1024], P('freq', 'sx', 'sy'), may hold values from 0.1 to 0.25
- frontal_inverse: bfloat16 [4, 4, 4, 1024, 1024], P('freq', 'sx', 'sy'), may hold values from -0.2 to 1.2
Outputs:
- solution: float32 [4, 4, 4, 1024, 128], P('freq', 'sx', 'sy')
- residual_total: float32 [], replicated
Inputs may be any that keep to these rules, and one draw needn't show every extreme that they name: In the 32 children of one grid position no owner appears more than 16 times; in every draw some owner appears exactly 16 times at some position.
All inputs are finite; a program needn't handle non-finite values.
Results may differ from a plain program's by a relative error of at most 0.0019.
Values may be sent and summed in bfloat16 or wider, within the bound.
A program may use at most 128 MiB of HBM per device.

v0:
```python
import jax
import jax.numpy as jnp
from jax import lax
from jax.sharding import PartitionSpec as P

SWEEPS = 2


def extended(block, sides, width):
    for axis, dim in sides:
        count = lax.axis_size(axis)
        forward = [(i, i + 1) for i in range(count - 1)]
        backward = [(target, source) for source, target in forward]
        low = lax.ppermute(
            lax.slice_in_dim(block, block.shape[dim] - width, None, axis=dim), axis, forward
        )
        high = lax.ppermute(lax.slice_in_dim(block, 0, width, axis=dim), axis, backward)
        block = jnp.concatenate([low, block, high], axis=dim)
    return block


def on_device(update_basis, update_coeff, owner, sep_rhs, coupling, frontal_inverse):
    f_local = update_basis.shape[0]
    sep_size = update_basis.shape[3]
    rhs_count = update_coeff.shape[3]
    columns = lax.axis_size("sx")
    owners = owner[:, 0]
    block_rows = f_local * sep_size
    owned_count = lax.axis_size("sx") * block_rows // block_rows
    candidates = jnp.arange(owned_count, dtype=jnp.int32)
    matches = (owners[:, None] == candidates[None, :]).astype(jnp.bfloat16)
    masked = matches.T[:, None, :, None, None] * update_coeff[None]
    products = jnp.einsum(
        "fcrs,jfcrn->jfsn", update_basis, masked, preferred_element_type=jnp.float32
    )
    summed = lax.psum_scatter(
        products.reshape(lax.axis_size("sx") * block_rows, rhs_count),
        "sx",
        scatter_dimension=0,
        tiled=True,
    )
    contribution = summed.reshape(f_local, sep_size, rhs_count)
    right_side = sep_rhs[:, 0, 0].astype(jnp.float32) - contribution
    inverse_block = frontal_inverse[:, 0, 0]
    coupling_rows = coupling[:, 0, 0]

    def apply_inverse(field):
        return jnp.einsum(
            "fst,ftn->fsn",
            inverse_block,
            field.astype(jnp.bfloat16),
            preferred_element_type=jnp.float32,
        )

    solution = apply_inverse(right_side)
    residual = right_side
    for sweep_index in range(SWEEPS):
        padded = extended(solution[:, None, None], (("sx", 1), ("sy", 2)), 1)
        beside = coupling_rows[:, 0, :, None] * padded[:, 0, 1]
        beside = beside + coupling_rows[:, 1, :, None] * padded[:, 2, 1]
        beside = beside + coupling_rows[:, 2, :, None] * padded[:, 1, 0]
        beside = beside + coupling_rows[:, 3, :, None] * padded[:, 1, 2]
        residual = right_side - solution + beside
        solution = solution + apply_inverse(residual)
    freq_ids = lax.axis_index("freq") * f_local + jnp.arange(f_local, dtype=jnp.int32) + 1
    weights = freq_ids.astype(jnp.float32) ** 2
    local_sum = jnp.sum(weights * jnp.sum(residual * residual, axis=(1, 2)))
    weighted_sum = lax.psum(local_sum, ("sx", "sy", "freq"))
    entries = float(
        f_local * lax.axis_size("freq") * columns * lax.axis_size("sy") * sep_size * rhs_count
    )
    residual_total = jnp.sqrt(weighted_sum / entries + 1e-06)
    return (solution[:, None, None], residual_total)


def solution(mesh):
    return jax.shard_map(
        on_device,
        mesh=mesh,
        in_specs=(
            P("freq", ("sx", "sy"), None, None),
            P("freq", ("sx", "sy"), None, None),
            P(("sx", "sy"), None),
            P("freq", "sx", "sy", None, None),
            P("freq", "sx", "sy", None, None),
            P("freq", "sx", "sy", None, None),
        ),
        out_specs=(P("freq", "sx", "sy", None, None), P()),
        check_vma=False,
    )
```

profile of v0, /device:TPU:0, one launch (start us, length us, event | category | flops | bytes accessed | tf_op | source)
XLA Modules:
  0.0 382.1 jit_solution(11093522134701189711)
XLA Ops:
  7.2 0.0 reduce-scatter.2.cloned.1.call-start
  7.2 0.7 fusion.49
  7.9 6.8 %fusion.8 = f32[4,2,1024,128]{2,3,0,1:T(8,128)} fusion(bf16[2,32,32,1024]{3,2,1,0:T(8,128)(2,1)} %param.6, bf16[2,32,32,128]{3,2,1,0:T(8,128)(2,1)} %param.7, bf16[4,32]{1,0:T(4,128)(2,1)S(1)} %fusion.49), kind=kOutput, calls=%fused_computation.10 | convolution fusion | flops 2148532224 | bytes 8913152 | tf_op jit(solution)/shard_map/fcrs,jfcrn->jfsn/dot_general | solution.py:33
  14.7 5.3 %copy.11 = f32[4,2,1024,128]{3,2,1,0:T(8,128)} copy(f32[4,2,1024,128]{2,3,0,1:T(8,128)} %fusion.8) | data formatting | bytes 8388608 | tf_op jit(solution)/shard_map/fcrs,jfcrn->jfsn/transpose | solution.py:33
  20.0 0.0 copy-start.4
  20.0 0.0 reduce-scatter.2.cloned.1.call-update
  20.0 1.0 copy-done.4
  21.0 0.2 copy.10
  21.3 54.3 %reduce-scatter.2.cloned.1.call-done = f32[2048,128]{1,0:T(8,128)} async-done(((f32[8192,128]{1,0:T(8,128)}), f32[2048,128]{1,0:T(8,128)}) %reduce-scatter.2.cloned.1.call-update) | async-done | bytes 1048592 | tf_op jit(solution)/shard_map/reduce_scatter | solution.py:36
  75.6 1.6 copy.12
  77.1 3.7 fusion.6
  80.8 0.0 copy-start.5
  80.9 0.0 copy-start
  80.9 3.6 collective-permute-start
  84.5 1.3 collective-permute-start.1
  85.8 21.0 %collective-permute-done = f32[2,1,1,1024,128]{3,4,0,2,1:T(8,128)S(1)} collective-permute-done((f32[2,1,1,1024,128]{3,4,0,2,1:T(8,128)S(1)}, f32[2,1,1,1024,128]{3,4,0,2,1:T(8,128)S(1)}, u32[]{:S(2)}, u32[]{:S(2)}) %collective-permute-start) | collective-permute-done | bytes 1048608 | tf_op jit(solution)/shard_map/ppermute | solution.py:14
  106.8 24.4 %collective-permute-done.1 = f32[2,1,1,1024,128]{3,4,0,2,1:T(8,128)S(1)} collective-permute-done((f32[2,1,1,1024,128]{3,4,0,2,1:T(8,128)S(1)}, f32[2,1,1,1024,128]{3,4,0,2,1:T(8,128)S(1)}, u32[]{:S(2)}, u32[]{:S(2)}) %collective-permute-start.1) | collective-permute-done | bytes 1048608 | tf_op jit(solution)/shard_map/ppermute | solution.py:17
  131.2 0.2 pad_maximum_fusion
  131.4 3.6 collective-permute-start.2
  135.0 1.3 collective-permute-start.3
  136.3 0.0 copy-done.5
  136.4 64.9 %collective-permute-done.2 = f32[2,3,1,1024,128]{3,4,0,2,1:T(8,128)S(1)} collective-permute-done((f32[2,3,1,1024,128]{3,4,0,2,1:T(8,128)S(1)}, f32[2,3,1,1024,128]{3,4,0,2,1:T(8,128)S(1)}, u32[]{:S(2)}, u32[]{:S(2)}) %collective-permute-start.2) | collective-permute-done | bytes 3145760 | tf_op jit(solution)/shard_map/ppermute | solution.py:14
  201.3 4.3 %collective-permute-done.3 = f32[2,3,1,1024,128]{3,4,0,2,1:T(8,128)S(1)} collective-permute-done((f32[2,3,1,1024,128]{3,4,0,2,1:T(8,128)S(1)}, f32[2,3,1,1024,128]{3,4,0,2,1:T(8,128)S(1)}, u32[]{:S(2)}, u32[]{:S(2)}) %collective-permute-start.3) | collective-permute-done | bytes 3145760 | tf_op jit(solution)/shard_map/ppermute | solution.py:17
  205.6 0.0 copy-done
  205.6 1.7 fusion.15
  207.3 2.6 collective-permute-start.4
  210.0 1.3 collective-permute-start.5
  211.3 19.0 %collective-permute-done.4 = f32[2,1,1,1024,128]{3,4,0,2,1:T(8,128)S(1)} collective-permute-done((f32[2,1,1,1024,128]{3,4,0,2,1:T(8,128)S(1)}, f32[2,1,1,1024,128]{3,4,0,2,1:T(8,128)S(1)}, u32[]{:S(2)}, u32[]{:S(2)}) %collective-permute-start.4) | collective-permute-done | bytes 1048608 | tf_op jit(solution)/shard_map/ppermute | solution.py:14
  230.2 0.0 copy-start.2
  230.2 23.2 %collective-permute-done.5 = f32[2,1,1,1024,128]{3,4,0,2,1:T(8,128)S(1)} collective-permute-done((f32[2,1,1,1024,128]{3,4,0,2,1:T(8,128)S(1)}, f32[2,1,1,1024,128]{3,4,0,2,1:T(8,128)S(1)}, u32[]{:S(2)}, u32[]{:S(2)}) %collective-permute-start.5) | collective-permute-done | bytes 1048608 | tf_op jit(solution)/shard_map/ppermute | solution.py:17
  253.4 0.0 copy-done.2
  253.4 0.0 copy-start.3
  253.4 2.0 pad_maximum_fusion.1
  255.5 0.0 copy-done.3
  255.5 4.8 %collective-permute-start.6 = (f32[2,3,1,1024,128]{3,4,0,2,1:T(8,128)}, f32[2,3,1,1024,128]{3,4,0,2,1:T(8,128)}, u32[]{:S(2)}, u32[]{:S(2)}) collective-permute-start(f32[2,3,1,1024,128]{3,4,0,2,1:T(8,128)} %pad_maximum_fusion.1), channel_id=1, source_target_pairs={{0,2},{2,4},{4,6},{1,3},{3,5},{5,7},{8,10},{10,12},{12,14},{9,11},... | collective-permute-start | bytes 9437192 | tf_op jit(solution)/shard_map/ppermute | solution.py:14
  260.3 1.3 collective-permute-start.7
  261.6 0.0 copy-start.1
  261.6 61.9 %collective-permute-done.6 = f32[2,3,1,1024,128]{3,4,0,2,1:T(8,128)} collective-permute-done((f32[2,3,1,1024,128]{3,4,0,2,1:T(8,128)}, f32[2,3,1,1024,128]{3,4,0,2,1:T(8,128)}, u32[]{:S(2)}, u32[]{:S(2)}) %collective-permute-start.6) | collective-permute-done | bytes 3145760 | tf_op jit(solution)/shard_map/ppermute | solution.py:14
  323.6 5.8 %collective-permute-done.7 = f32[2,3,1,1024,128]{3,4,0,2,1:T(8,128)} collective-permute-done((f32[2,3,1,1024,128]{3,4,0,2,1:T(8,128)}, f32[2,3,1,1024,128]{3,4,0,2,1:T(8,128)}, u32[]{:S(2)}, u32[]{:S(2)}) %collective-permute-start.7) | collective-permute-done | bytes 3145760 | tf_op jit(solution)/shard_map/ppermute | solution.py:17
  329.3 2.8 multiply_reduce_fusion
  332.2 0.0 copy-done.1
  332.2 1.5 fusion.24
  333.7 0.6 multiply_reduce_fusion.1
  334.3 1.3 copy.13
  335.6 37.8 %psum.7 = f32[]{:T(128)} all-reduce(f32[]{:T(128)} %multiply_reduce_fusion.1), channel_id=1, replica_groups=mesh['sx'=4,'sy'=4,'freq'=2] {'sx','sy','freq'}, use_global_device_ids=true, to_apply=%region_3.0 | all-reduce | flops 1 | bytes 8 | tf_op jit(solution)/shard_map/psum | solution.py:68
  (3 shorter events, 0.0 us)
Async XLA Ops:
  7.2 68.4 %reduce-scatter.2.cloned.1.call-start = ((), (), s32[]{:S(2)}) async-start(), calls=%async_computation.1 | async-start | bytes 5242880 | tf_op jit(solution)/shard_map/reduce_scatter | solution.py:36
  20.0 1.0 copy-start.4
  80.8 55.5 %copy-start.5 = (f32[2,1,1,4,1024]{4,3,2,1,0:T(4,128)S(1)}, f32[2,1,1,4,1024]{4,3,2,1,0:T(4,128)}, u32[]{:S(2)}) copy-start(f32[2,1,1,4,1024]{4,3,2,1,0:T(4,128)} %param.10) | copy-start | bytes 98308
  80.9 124.8 %copy-start = (bf16[2,1,1,1024,1024]{4,3,2,1,0:T(8,128)(2,1)S(1)}, bf16[2,1,1,1024,1024]{4,3,2,1,0:T(8,128)(2,1)}, u32[]{:S(2)}) copy-start(bf16[2,1,1,1024,1024]{4,3,2,1,0:T(8,128)(2,1)} %param.11) | copy-start | bytes 12582916
  80.9 25.9 %collective-permute-start = (f32[2,1,1,1024,128]{3,4,0,2,1:T(8,128)S(1)}, f32[2,1,1,1024,128]{3,4,0,2,1:T(8,128)S(1)}, u32[]{:S(2)}, u32[]{:S(2)}) collective-permute-start(f32[2,1,1,1024,128]{3,4,0,2,1:T(8,128)S(1)} %bitcast.141), channel_id=1, source_target_pairs={{0,8},{8,16},{16,24},{1,9},{9,17},{17,25},{2,10},{10,18},{18,26},{... | collective-permute-start | bytes 3145736 | tf_op jit(solution)/shard_map/ppermute | solution.py:14
  84.5 46.7 %collective-permute-start.1 = (f32[2,1,1,1024,128]{3,4,0,2,1:T(8,128)S(1)}, f32[2,1,1,1024,128]{3,4,0,2,1:T(8,128)S(1)}, u32[]{:S(2)}, u32[]{:S(2)}) collective-permute-start(f32[2,1,1,1024,128]{3,4,0,2,1:T(8,128)S(1)} %bitcast.142), channel_id=1, source_target_pairs={{8,0},{16,8},{24,16},{9,1},{17,9},{25,17},{10,2},{18,10},{26,18},{... | collective-permute-start | bytes 3145736 | tf_op jit(solution)/shard_map/ppermute | solution.py:17
  131.4 69.9 %collective-permute-start.2 = (f32[2,3,1,1024,128]{3,4,0,2,1:T(8,128)S(1)}, f32[2,3,1,1024,128]{3,4,0,2,1:T(8,128)S(1)}, u32[]{:S(2)}, u32[]{:S(2)}) collective-permute-start(f32[2,3,1,1024,128]{3,4,0,2,1:T(8,128)S(1)} %pad_maximum_fusion), channel_id=1, source_target_pairs={{0,2},{2,4},{4,6},{1,3},{3,5},{5,7},{8,10},{10,12},{12,14},{9,11},... | collective-permute-start | bytes 9437192 | tf_op jit(solution)/shard_map/ppermute | solution.py:14
  135.0 70.6 %collective-permute-start.3 = (f32[2,3,1,1024,128]{3,4,0,2,1:T(8,128)S(1)}, f32[2,3,1,1024,128]{3,4,0,2,1:T(8,128)S(1)}, u32[]{:S(2)}, u32[]{:S(2)}) collective-permute-start(f32[2,3,1,1024,128]{3,4,0,2,1:T(8,128)S(1)} %pad_maximum_fusion), channel_id=1, source_target_pairs={{2,0},{4,2},{6,4},{3,1},{5,3},{7,5},{10,8},{12,10},{14,12},{11,9},... | collective-permute-start | bytes 9437192 | tf_op jit(solution)/shard_map/ppermute | solution.py:17
  207.3 22.9 %collective-permute-start.4 = (f32[2,1,1,1024,128]{3,4,0,2,1:T(8,128)S(1)}, f32[2,1,1,1024,128]{3,4,0,2,1:T(8,128)S(1)}, u32[]{:S(2)}, u32[]{:S(2)}) collective-permute-start(f32[2,1,1,1024,128]{3,4,0,2,1:T(8,128)S(1)} %bitcast.138), channel_id=1, source_target_pairs={{0,8},{8,16},{16,24},{1,9},{9,17},{17,25},{2,10},{10,18},{18,26},{... | collective-permute-start | bytes 3145736 | tf_op jit(solution)/shard_map/ppermute | solution.py:14
  210.0 43.5 %collective-permute-start.5 = (f32[2,1,1,1024,128]{3,4,0,2,1:T(8,128)S(1)}, f32[2,1,1,1024,128]{3,4,0,2,1:T(8,128)S(1)}, u32[]{:S(2)}, u32[]{:S(2)}) collective-permute-start(f32[2,1,1,1024,128]{3,4,0,2,1:T(8,128)S(1)} %bitcast.139), channel_id=1, source_target_pairs={{8,0},{16,8},{24,16},{9,1},{17,9},{25,17},{10,2},{18,10},{26,18},{... | collective-permute-start | bytes 3145736 | tf_op jit(solution)/shard_map/ppermute | solution.py:17
  230.2 23.2 %copy-start.2 = (f32[2,1,1,1024,128]{3,4,0,2,1:T(8,128)}, f32[2,1,1,1024,128]{3,4,0,2,1:T(8,128)S(1)}, u32[]{:S(2)}) copy-start(f32[2,1,1,1024,128]{3,4,0,2,1:T(8,128)S(1)} %collective-permute-done.4) | copy-start | bytes 3145732
  253.4 2.1 copy-start.3
  255.5 68.1 %collective-permute-start.6 = (f32[2,3,1,1024,128]{3,4,0,2,1:T(8,128)}, f32[2,3,1,1024,128]{3,4,0,2,1:T(8,128)}, u32[]{:S(2)}, u32[]{:S(2)}) collective-permute-start(f32[2,3,1,1024,128]{3,4,0,2,1:T(8,128)} %pad_maximum_fusion.1), channel_id=1, source_target_pairs={{0,2},{2,4},{4,6},{1,3},{3,5},{5,7},{8,10},{10,12},{12,14},{9,11},... | collective-permute-start | bytes 9437192 | tf_op jit(solution)/shard_map/ppermute | solution.py:14
  260.3 69.0 %collective-permute-start.7 = (f32[2,3,1,1024,128]{3,4,0,2,1:T(8,128)}, f32[2,3,1,1024,128]{3,4,0,2,1:T(8,128)}, u32[]{:S(2)}, u32[]{:S(2)}) collective-permute-start(f32[2,3,1,1024,128]{3,4,0,2,1:T(8,128)} %pad_maximum_fusion.1), channel_id=1, source_target_pairs={{2,0},{4,2},{6,4},{3,1},{5,3},{7,5},{10,8},{12,10},{14,12},{11,9},... | collective-permute-start | bytes 9437192 | tf_op jit(solution)/shard_map/ppermute | solution.py:17
  261.6 70.6 %copy-start.1 = (bf16[2,1,1,1024,1024]{4,3,2,1,0:T(8,128)(2,1)S(1)}, bf16[2,1,1,1024,1024]{4,3,2,1,0:T(8,128)(2,1)}, u32[]{:S(2)}) copy-start(bf16[2,1,1,1024,1024]{4,3,2,1,0:T(8,128)(2,1)} %param.11) | copy-start | bytes 12582916
Sparse Core Ops, SparseCore 0:
  20.1 55.3 reduce-scatter.1
where the time goes:
time: 383 us; the launch traced here: 382 us
  waiting for transfers between devices  279 us (73%)
  blocking collectives  37.8 us (10%)
  starting transfers between devices  19.9 us (5%)
  between operations  16 us (4%)
  matrix products  13.7 us (4%)
  local copies, waits for them, and re-layouts  9.49 us (2%)
  other arithmetic  6.36 us (2%)
    ppermute x4, waiting for transfers between devices, extended(): lax.ppermute(lax.slice_in_dim(block, block.shape[dim] - width, None, axis...  167 us
    ppermute x4, waiting for transfers between devices, extended(): lax.ppermute(lax.slice_in_dim(block, 0, width, axis=dim), axis, backward)  57.7 us
    reduce_scatter x1, waiting for transfers between devices, on_device(): lax.psum_scatter(products.reshape(lax.axis_size('sx') * block_rows, rhs_c...  54.3 us
    psum x1, blocking collectives, on_device(): weighted_sum = lax.psum(local_sum, ('sx', 'sy', 'freq'))  37.8 us
    ppermute x4, starting transfers between devices, extended(): lax.ppermute(lax.slice_in_dim(block, block.shape[dim] - width, None, axis...  14.7 us
  transfers between devices with their start and end apart: 9, of which 9 were waited for; matrix products, arithmetic and copies ran while one was open for 0% of the time, Pallas kernels for 0%

commit v1 on v0

v1 whole, which is shorter than its diff:
```python
import functools
import jax
import jax.numpy as jnp
from jax import lax
from jax.experimental import pallas as pl
from jax.experimental.pallas import tpu as pltpu
from jax.sharding import PartitionSpec as P

SWEEPS = 2
BLOCK = 256
GROUP = 512
MESH = pl.DeviceIdType.MESH
F32 = jnp.float32
BF16 = jnp.bfloat16


def kernel(
    sizes,
    basis_hbm, coeff_ref, owner_ref, rhs_ref, coupling_ref, inverse_hbm,
    out_ref, total_ref,
    basis_ref, inverse_ref, masked_ref, sent_ref, got_ref, own_ref, right_ref, field_ref,
    halo_out_ref, halo_in_ref, coupling_t_ref, sums_a_ref, sums_b_ref,
    basis_sem, inverse_sem, sent_sem, got_sem, halo_out_sem, halo_in_sem,
    a_send_sem, a_recv_sem, b_send_sem, b_recv_sem,
):
    n_x, n_y, n_f, entries = sizes
    f_local, depth, sep = basis_ref.shape
    rhs_count = rhs_ref.shape[2]
    children = owner_ref.shape[0]
    rank = depth // children
    blocks = sep // BLOCK
    paired = n_x == 4
    x = lax.axis_index("sx")
    y = lax.axis_index("sy")
    z = lax.axis_index("freq")

    loads = []
    for f in range(f_local):
        loads.append(pltpu.make_async_copy(basis_hbm.at[f], basis_ref.at[f], basis_sem.at[f]))
    inverse_loads = []
    for f in range(f_local):
        inverse_loads.append(
            pltpu.make_async_copy(inverse_hbm.at[f], inverse_ref.at[f], inverse_sem.at[f])
        )
    for copy in loads + inverse_loads:
        copy.start()

    barrier = pltpu.get_barrier_semaphore()
    count = 0
    for dx in range(n_x):
        for dz in range(n_f):
            if dx or dz:
                pl.semaphore_signal(
                    barrier, inc=1, device_id=(lax.rem(x + dx, n_x), y, lax.rem(z + dz, n_f)),
                    device_id_type=MESH,
                )
                count += 1
    for dy in range(1, n_y):
        pl.semaphore_signal(
            barrier, inc=1, device_id=(x, lax.rem(y + dy, n_y), z), device_id_type=MESH
        )
        count += 1

    if paired:
        px, py = lax.rem(x, 2), x // 2
        owners = [(1 - py) * 2 + 1 - px, py * 2 + 1 - px, (1 - py) * 2 + px, x]
    else:
        owners = [lax.rem(x + k, n_x) for k in range(1, n_x)] + [x]

    def mask(f):
        def one_child(c, carry):
            mine = owner_ref[pl.ds(c, 1), :]
            rows = pl.ds(pl.multiple_of(c * rank, rank), rank)
            values = coeff_ref[f, rows, :]
            for k, who in enumerate(owners):
                keep = jnp.where(mine == who, 1.0, 0.0).astype(F32)
                keep = jnp.broadcast_to(keep, (rank, rhs_count)).astype(BF16)
                masked_ref[f, rows, k * rhs_count:(k + 1) * rhs_count] = values * keep
            return carry

        lax.fori_loop(0, children, one_child, 0, unroll=4)

    pending = []

    def remote(src, dst, send, recv, device):
        return pltpu.make_async_remote_copy(
            src_ref=src, dst_ref=dst, send_sem=send, recv_sem=recv,
            device_id=device, device_id_type=MESH,
        )

    def sum_copy(f, k, b):
        rows = pl.ds(b * BLOCK, BLOCK)
        return remote(
            sent_ref.at[k, f, rows], got_ref.at[k, f, rows],
            sent_sem.at[k, f, b], got_sem.at[k, f, b], (owners[k], y, z),
        )

    for f in range(f_local):
        mask(f)
        loads[f].wait()
        if f == 0:
            pl.semaphore_wait(barrier, count)
        for b in range(blocks):
            rows = pl.ds(b * BLOCK, BLOCK)
            part = basis_ref[f, :, b * BLOCK:(b + 1) * BLOCK]
            for low in range(0, n_x * rhs_count, GROUP):
                high = min(low + GROUP, n_x * rhs_count)
                sums = lax.dot_general(
                    part, masked_ref[f, :, low:high], (((0,), (0,)), ((), ())),
                    preferred_element_type=F32,
                )
                for k in range(low // rhs_count, high // rhs_count):
                    at = k * rhs_count - low
                    piece = sums[:, at:at + rhs_count]
                    if k == n_x - 1:
                        own_ref[f, rows, :] = rhs_ref[f, rows, :].astype(F32) - piece
                    else:
                        sent_ref[k, f, rows, :] = piece.astype(BF16)
                        copy = sum_copy(f, k, b)
                        copy.start()
                        pending.append((None, copy))

    both = jnp.concatenate([coupling_ref[f] for f in range(f_local)], axis=0)
    coupling_t_ref[...] = both.T

    edges = ((x == 0, 0), (x == n_x - 1, 1), (y == 0, 2), (y == n_y - 1, 3))
    for missing, side in edges:
        @pl.when(missing)
        def _():
            for sweep in range(SWEEPS):
                for f in range(f_local):
                    halo_in_ref[sweep, f, side] = jnp.zeros((sep, rhs_count), BF16)

    def halo_copy(sweep, f, b, way, source, device):
        rows = pl.ds(b * BLOCK, BLOCK)
        return remote(
            source, halo_in_ref.at[sweep, f, way, rows],
            halo_out_sem.at[sweep, f, way, b], halo_in_sem.at[sweep, f, way, b], device,
        )

    up, down = x < n_x - 1, x > 0
    if paired:
        up = jnp.logical_and(up, x != 1)
        down = jnp.logical_and(down, x != 2)

    def send_halo(sweep, f, b):
        source = halo_out_ref.at[sweep, f, pl.ds(b * BLOCK, BLOCK)]
        for way, test, device in (
            (0, up, (x + 1, y, z)), (1, down, (x - 1, y, z)),
            (2, y < n_y - 1, (x, y + 1, z)), (3, y > 0, (x, y - 1, z)),
        ):
            copy = halo_copy(sweep, f, b, way, source, device)
            pl.when(test)(copy.start)
            pending.append((test, copy))

    def wait_halo(sweep, f, b, way):
        source = halo_out_ref.at[sweep, f, pl.ds(b * BLOCK, BLOCK)]
        test = (x > 0, x < n_x - 1, y > 0, y < n_y - 1)[way]
        copy = halo_copy(sweep, f, b, way, source, (x, y, z))
        pl.when(test)(copy.wait_recv)

    def pass_on(sweep, f, b):
        rows = pl.ds(b * BLOCK, BLOCK)
        for test, held, way, target in ((x == 0, 1, 0, 2), (x == 3, 0, 1, 1)):
            source = halo_in_ref.at[sweep, f, held, rows]
            copy = remote(
                source, halo_in_ref.at[sweep, f, way, rows],
                halo_out_sem.at[sweep, f, held, b], halo_in_sem.at[sweep, f, way, b],
                (target, y, z),
            )
            pl.when(test)(copy.start)
            pending.append((test, copy))

    def apply_inverse(f, sweep, first):
        for b in range(blocks):
            rows = pl.ds(b * BLOCK, BLOCK)
            value = jnp.dot(inverse_ref[f, rows, :], field_ref[f], preferred_element_type=F32)
            if not first:
                value = out_ref[f, rows, :] + value
            out_ref[f, rows, :] = value
            if sweep < SWEEPS:
                halo_out_ref[sweep, f, rows, :] = value.astype(BF16)
                send_halo(sweep, f, b)

    for f in range(f_local):
        for b in range(blocks):
            rows = pl.ds(b * BLOCK, BLOCK)
            value = own_ref[f, rows, :]
            for k in range(n_x - 1):
                sum_copy(f, k, b).wait_recv()
                value = value - got_ref[k, f, rows, :].astype(F32)
            right_ref[f, rows, :] = value
            field_ref[f, rows, :] = value.astype(BF16)
        inverse_loads[f].wait()
        apply_inverse(f, 0, True)

    weighted = jnp.zeros((8, rhs_count), F32)
    for sweep in range(SWEEPS):
        for f in range(f_local):
            for b in range(blocks):
                wait_halo(sweep, f, b, 0)
                wait_halo(sweep, f, b, 1)
                if paired:
                    pass_on(sweep, f, b)
            squares = jnp.zeros((8, rhs_count), F32)
            for b in range(blocks):
                wait_halo(sweep, f, b, 2)
                wait_halo(sweep, f, b, 3)
                rows = pl.ds(b * BLOCK, BLOCK)
                beside = jnp.zeros((BLOCK, rhs_count), F32)
                for side in range(4):
                    column = 4 * f + side
                    beside = beside + (
                        coupling_t_ref[rows, column:column + 1]
                        * halo_in_ref[sweep, f, side, rows, :].astype(F32)
                    )
                residual = right_ref[f, rows, :] - out_ref[f, rows, :] + beside
                field_ref[f, rows, :] = residual.astype(BF16)
                if sweep == SWEEPS - 1:
                    squares = squares + jnp.sum(
                        (residual * residual).reshape(BLOCK // 8, 8, rhs_count), axis=0
                    )
            if sweep == SWEEPS - 1:
                weight = (z * f_local + f + 1).astype(F32)
                weighted = weighted + (weight * weight) * squares
                if f == f_local - 1:
                    mine = x * n_f + z
                    sums_a_ref[mine] = weighted
                    for dx in range(n_x):
                        for dz in range(n_f):
                            if dx or dz:
                                k = dx * n_f + dz
                                copy = remote(
                                    sums_a_ref.at[mine], sums_a_ref.at[mine],
                                    a_send_sem.at[k], a_recv_sem.at[k],
                                    (lax.rem(x + dx, n_x), y, lax.rem(z + dz, n_f)),
                                )
                                copy.start()
                                pending.append((None, copy))
            apply_inverse(f, sweep + 1, False)

    for k in range(1, n_x * n_f):
        dx, dz = k // n_f, k % n_f
        source = lax.rem(x + n_x - dx, n_x) * n_f + lax.rem(z + n_f - dz, n_f)
        remote(
            sums_a_ref.at[source], sums_a_ref.at[source], a_send_sem.at[k], a_recv_sem.at[k],
            (x, y, z),
        ).wait_recv()
    part = sums_a_ref[0]
    for k in range(1, n_x * n_f):
        part = part + sums_a_ref[k]
    sums_b_ref[y] = part
    for dy in range(1, n_y):
        copy = remote(
            sums_b_ref.at[y], sums_b_ref.at[y], b_send_sem.at[dy], b_recv_sem.at[dy],
            (x, lax.rem(y + dy, n_y), z),
        )
        copy.start()
        pending.append((None, copy))
    for dy in range(1, n_y):
        source = lax.rem(y + n_y - dy, n_y)
        remote(
            sums_b_ref.at[source], sums_b_ref.at[source], b_send_sem.at[dy], b_recv_sem.at[dy],
            (x, y, z),
        ).wait_recv()
    part = sums_b_ref[0]
    for k in range(1, n_y):
        part = part + sums_b_ref[k]
    whole = jnp.sum(jnp.sum(part, axis=1, keepdims=True), axis=0, keepdims=True)
    total_ref[...] = jnp.sqrt(whole / entries + 1e-06)

    for test, copy in pending:
        if test is None:
            copy.wait_send()
        else:
            pl.when(test)(copy.wait_send)


def on_device(sizes, update_basis, update_coeff, owner, sep_rhs, coupling, frontal_inverse):
    f_local, children, rank, sep = update_basis.shape
    rhs_count = update_coeff.shape[3]
    depth = children * rank
    n_x, n_y, n_f = sizes
    blocks = sep // BLOCK
    entries = float(f_local * n_f * n_x * n_y * sep * rhs_count)
    vmem = pl.BlockSpec(memory_space=pltpu.VMEM)
    anywhere = pl.BlockSpec(memory_space=pl.ANY)
    solved, total = pl.pallas_call(
        functools.partial(kernel, (n_x, n_y, n_f, entries)),
        out_shape=(
            jax.ShapeDtypeStruct((f_local, sep, rhs_count), F32),
            jax.ShapeDtypeStruct((1, 1), F32),
        ),
        in_specs=[anywhere, vmem, vmem, vmem, vmem, anywhere],
        out_specs=(vmem, vmem),
        scratch_shapes=[
            pltpu.VMEM((f_local, depth, sep), BF16),
            pltpu.VMEM((f_local, sep, sep), BF16),
            pltpu.VMEM((f_local, depth, n_x * rhs_count), BF16),
            pltpu.VMEM((n_x - 1, f_local, sep, rhs_count), BF16),
            pltpu.VMEM((n_x - 1, f_local, sep, rhs_count), BF16),
            pltpu.VMEM((f_local, sep, rhs_count), F32),
            pltpu.VMEM((f_local, sep, rhs_count), F32),
            pltpu.VMEM((f_local, sep, rhs_count), BF16),
            pltpu.VMEM((SWEEPS, f_local, sep, rhs_count), BF16),
            pltpu.VMEM((SWEEPS, f_local, 4, sep, rhs_count), BF16),
            pltpu.VMEM((sep, 4 * f_local), F32),
            pltpu.VMEM((n_x * n_f, 8, rhs_count), F32),
            pltpu.VMEM((n_y, 8, rhs_count), F32),
            pltpu.SemaphoreType.DMA((f_local,)),
            pltpu.SemaphoreType.DMA((f_local,)),
            pltpu.SemaphoreType.DMA((n_x - 1, f_local, blocks)),
            pltpu.SemaphoreType.DMA((n_x - 1, f_local, blocks)),
            pltpu.SemaphoreType.DMA((SWEEPS, f_local, 4, blocks)),
            pltpu.SemaphoreType.DMA((SWEEPS, f_local, 4, blocks)),
            pltpu.SemaphoreType.DMA((n_x * n_f,)),
            pltpu.SemaphoreType.DMA((n_x * n_f,)),
            pltpu.SemaphoreType.DMA((n_y,)),
            pltpu.SemaphoreType.DMA((n_y,)),
        ],
        compiler_params=pltpu.CompilerParams(
            collective_id=0, has_side_effects=True, vmem_limit_bytes=56 * 2**20
        ),
    )(
        update_basis.reshape(f_local, depth, sep),
        update_coeff.reshape(f_local, depth, rhs_count),
        owner,
        sep_rhs[:, 0, 0],
        coupling[:, 0, 0],
        frontal_inverse[:, 0, 0],
    )
    return (solved[:, None, None], total.reshape(()))


def solution(mesh):
    sizes = (mesh.shape["sx"], mesh.shape["sy"], mesh.shape["freq"])
    return jax.shard_map(
        functools.partial(on_device, sizes),
        mesh=mesh,
        in_specs=(
            P("freq", ("sx", "sy"), None, None),
            P("freq", ("sx", "sy"), None, None),
            P(("sx", "sy"), None),
            P("freq", "sx", "sy", None, None),
            P("freq", "sx", "sy", None, None),
            P("freq", "sx", "sy", None, None),
        ),
        out_specs=(P("freq", "sx", "sy", None, None), P()),
        check_vma=False,
    )
```

time: 383 us -> 74.2 us (0.19)
  waiting for transfers between devices: 279 us -> 0 us
  Pallas kernels: 0 us -> 68.1 us
  blocking collectives: 37.8 us -> 0 us
  starting transfers between devices: 19.9 us -> 0 us
  matrix products: 13.7 us -> 0 us
  between operations: 16 us -> 2.33 us
  other arithmetic: 6.36 us -> 0 us
  local copies, waits for them, and re-layouts: 9.49 us -> 3.6 us
    ppermute x8 -> x0, waiting for transfers between devices: 225 us -> none  [the longest x4 167 us: extended(): lax.ppermute(lax.slice_in_dim(block, block.shape[dim] - width, None, axis...]
    pallas_call x0 -> x1, Pallas kernels: none -> 68.1 us  [on_device(): pl.pallas_call(functools.partial(kernel, (n_x, n_y, n_f, entries)), out_s...]
    reduce_scatter x1 -> x0, waiting for transfers between devices: 54.3 us -> none  [on_device(): lax.psum_scatter(products.reshape(lax.axis_size('sx') * block_rows, rhs_c...]
    psum x1 -> x0, blocking collectives: 37.8 us -> none  [on_device(): weighted_sum = lax.psum(local_sum, ('sx', 'sy', 'freq'))]
    ppermute x8 -> x0, starting transfers between devices: 19.8 us -> none  [the longest x4 14.7 us: extended(): lax.ppermute(lax.slice_in_dim(block, block.shape[dim] - width, None, axis...]
    dot_general x4 -> x0, matrix products: 13.7 us -> none  [the longest x3 6.93 us: apply_inverse(): jnp.einsum('fst,ftn->fsn', inverse_block, field.astype(jnp.bfloat16), pre...]
    transpose x1 -> x0, local copies, waits for them, and re-layouts: 5.32 us -> none  [on_device(): jnp.einsum('fcrs,jfcrn->jfsn', update_basis, masked, preferred_element_ty...]
  transfers between devices with their start and end apart: 9 -> 0, of which waited for: 9 -> 0; matrix products, arithmetic and copies ran while one was open for 0% -> 0% of each run, Pallas kernels for 0% -> 0%
where the time goes in v1:
time: 74.2 us; the launch traced here: 74 us
  Pallas kernels  68.1 us (92%)
  local copies, waits for them, and re-layouts  3.6 us (5%)
  between operations  2.33 us (3%)
    pallas_call x1, Pallas kernels, on_device(): pl.pallas_call(functools.partial(kernel, (n_x, n_y, n_f, entries)), out_s...  68.1 us
    unnamed x2, local copies, waits for them, and re-layouts  3.6 us

profile of v1, /device:TPU:0, one launch (start us, length us, event | category | flops | bytes accessed | tf_op | source)
XLA Modules:
  0.0 74.0 jit_solution(10292324050838186606)
XLA Ops:
  0.6 1.3 %copy.8.owner_ref = s32[32,1]{1,0:T(8,128)} copy(s32[32,1]{0,1:T(1,128)} %param.8) | data formatting | bytes 256 | tf_op args[2]
  2.0 68.1 %shard_map.77 = (f32[2,1024,128]{2,1,0:T(8,128)}, f32[1,1]{1,0:T(1,128)}) custom-call(bf16[2,1024,1024]{2,1,0:T(8,128)(2,1)} %bitcast.9, bf16[2,1024,128]{2,1,0:T(8,128)(2,1)} %bitcast.12, s32[32,1]{1,0:T(8,128)} %copy.8.owner_ref, bf16[2,1024,128]{2,1,0:T(8,128)(2,1)} %bitcast.13, f32[2,4,1024]{2,1,0:T(4,128)} %bitcast.14, bf16[2,1024,1024]{2,1,0:T(8,128)(2,1)} %bitcast.10), custom_call_target="tpu_custom_call" | custom-call | tf_op jit(solution)/shard_map/pallas_call | solution.py:288
  70.1 2.3 %copy.12 = f32[2,1,1,1024,128]{4,3,2,1,0:T(8,128)} copy(f32[2,1,1,1024,128]{4,3,2,1,0:T(8,128)} %bitcast.11) | data formatting | bytes 2097152

commit v2 on v1

--- a/solution.py
+++ b/solution.py
@@ -26,7 +26,7 @@
     n_x, n_y, n_f, entries = sizes
     f_local, depth, sep = basis_ref.shape
     rhs_count = rhs_ref.shape[2]
-    children = owner_ref.shape[0]
+    children = owner_ref.shape[1]
     rank = depth // children
     blocks = sep // BLOCK
     paired = n_x == 4
@@ -67,18 +67,18 @@
     else:
         owners = [lax.rem(x + k, n_x) for k in range(1, n_x)] + [x]
 
+    child_of = lax.broadcasted_iota(jnp.int32, (children, depth), 1) // rank
+    spread = (child_of == lax.broadcasted_iota(jnp.int32, (children, depth), 0)).astype(F32)
+    owner_rows = jnp.broadcast_to(owner_ref[...].astype(F32), (8, children))
+    owner_lanes = jnp.dot(
+        owner_rows.astype(BF16), spread.astype(BF16), preferred_element_type=F32
+    )[0:1, :]
+
     def mask(f):
-        def one_child(c, carry):
-            mine = owner_ref[pl.ds(c, 1), :]
-            rows = pl.ds(pl.multiple_of(c * rank, rank), rank)
-            values = coeff_ref[f, rows, :]
-            for k, who in enumerate(owners):
-                keep = jnp.where(mine == who, 1.0, 0.0).astype(F32)
-                keep = jnp.broadcast_to(keep, (rank, rhs_count)).astype(BF16)
-                masked_ref[f, rows, k * rhs_count:(k + 1) * rhs_count] = values * keep
-            return carry
-
-        lax.fori_loop(0, children, one_child, 0, unroll=4)
+        turned = coeff_ref[f].astype(F32).T
+        for k, who in enumerate(owners):
+            keep = jnp.where(owner_lanes == jnp.asarray(who).astype(F32), 1.0, 0.0)
+            masked_ref[f, k * rhs_count:(k + 1) * rhs_count, :] = (turned * keep).astype(BF16)
 
     pending = []
 
@@ -89,36 +89,34 @@
         )
 
     def sum_copy(f, k, b):
-        rows = pl.ds(b * BLOCK, BLOCK)
         return remote(
-            sent_ref.at[k, f, rows], got_ref.at[k, f, rows],
+            sent_ref.at[k, f, b], got_ref.at[k, f, b],
             sent_sem.at[k, f, b], got_sem.at[k, f, b], (owners[k], y, z),
         )
 
     for f in range(f_local):
         mask(f)
         loads[f].wait()
-        if f == 0:
-            pl.semaphore_wait(barrier, count)
         for b in range(blocks):
-            rows = pl.ds(b * BLOCK, BLOCK)
             part = basis_ref[f, :, b * BLOCK:(b + 1) * BLOCK]
             for low in range(0, n_x * rhs_count, GROUP):
                 high = min(low + GROUP, n_x * rhs_count)
-                sums = lax.dot_general(
-                    part, masked_ref[f, :, low:high], (((0,), (0,)), ((), ())),
-                    preferred_element_type=F32,
-                )
+                sums = jnp.dot(masked_ref[f, low:high, :], part, preferred_element_type=F32)
                 for k in range(low // rhs_count, high // rhs_count):
                     at = k * rhs_count - low
-                    piece = sums[:, at:at + rhs_count]
+                    piece = sums[at:at + rhs_count, :]
                     if k == n_x - 1:
-                        own_ref[f, rows, :] = rhs_ref[f, rows, :].astype(F32) - piece
+                        own_ref[f, b] = piece
                     else:
-                        sent_ref[k, f, rows, :] = piece.astype(BF16)
-                        copy = sum_copy(f, k, b)
-                        copy.start()
-                        pending.append((None, copy))
+                        sent_ref[k, f, b] = piece.astype(BF16)
+
+    pl.semaphore_wait(barrier, count)
+    for f in range(f_local):
+        for b in range(blocks):
+            for k in range(n_x - 1):
+                copy = sum_copy(f, k, b)
+                copy.start()
+                pending.append((None, copy))
 
     both = jnp.concatenate([coupling_ref[f] for f in range(f_local)], axis=0)
     coupling_t_ref[...] = both.T
@@ -185,10 +183,11 @@
     for f in range(f_local):
         for b in range(blocks):
             rows = pl.ds(b * BLOCK, BLOCK)
-            value = own_ref[f, rows, :]
+            value = own_ref[f, b]
             for k in range(n_x - 1):
                 sum_copy(f, k, b).wait_recv()
-                value = value - got_ref[k, f, rows, :].astype(F32)
+                value = value + got_ref[k, f, b].astype(F32)
+            value = rhs_ref[f, rows, :].astype(F32) - value.T
             right_ref[f, rows, :] = value
             field_ref[f, rows, :] = value.astype(BF16)
         inverse_loads[f].wait()
@@ -296,10 +295,10 @@
         scratch_shapes=[
             pltpu.VMEM((f_local, depth, sep), BF16),
             pltpu.VMEM((f_local, sep, sep), BF16),
-            pltpu.VMEM((f_local, depth, n_x * rhs_count), BF16),
-            pltpu.VMEM((n_x - 1, f_local, sep, rhs_count), BF16),
-            pltpu.VMEM((n_x - 1, f_local, sep, rhs_count), BF16),
-            pltpu.VMEM((f_local, sep, rhs_count), F32),
+            pltpu.VMEM((f_local, n_x * rhs_count, depth), BF16),
+            pltpu.VMEM((n_x - 1, f_local, blocks, rhs_count, BLOCK), BF16),
+            pltpu.VMEM((n_x - 1, f_local, blocks, rhs_count, BLOCK), BF16),
+            pltpu.VMEM((f_local, blocks, rhs_count, BLOCK), F32),
             pltpu.VMEM((f_local, sep, rhs_count), F32),
             pltpu.VMEM((f_local, sep, rhs_count), BF16),
             pltpu.VMEM((SWEEPS, f_local, sep, rhs_count), BF16),
@@ -324,7 +323,7 @@
     )(
         update_basis.reshape(f_local, depth, sep),
         update_coeff.reshape(f_local, depth, rhs_count),
-        owner,
+        owner.reshape(1, children),
         sep_rhs[:, 0, 0],
         coupling[:, 0, 0],
         frontal_inverse[:, 0, 0],

time: 74.2 us -> 74.7 us (level)
  Pallas kernels: 68.1 us -> 69.9 us
  local copies, waits for them, and re-layouts: 3.6 us -> 2.26 us
    pallas_call x1, Pallas kernels: 68.1 us -> 69.9 us  [on_device(): pl.pallas_call(functools.partial(kernel, (n_x, n_y, n_f, entries)), out_s...]
    unnamed x2 -> x1, local copies, waits for them, and re-layouts: 3.6 us -> 2.26 us
where the time goes in v2:
time: 74.7 us; the launch traced here: 74.5 us
  Pallas kernels  69.9 us (94%)
  between operations  2.33 us (3%)
  local copies, waits for them, and re-layouts  2.26 us (3%)
    pallas_call x1, Pallas kernels, on_device(): pl.pallas_call(functools.partial(kernel, (n_x, n_y, n_f, entries)), out_s...  69.9 us
    unnamed x1, local copies, waits for them, and re-layouts  2.26 us

profile of v2, /device:TPU:0, one launch (start us, length us, event | category | flops | bytes accessed | tf_op | source)
XLA Modules:
  0.0 74.5 jit_solution(2712671650452490149)
XLA Ops:
  0.6 69.9 %shard_map.77 = (f32[2,1024,128]{2,1,0:T(8,128)}, f32[1,1]{1,0:T(1,128)}) custom-call(bf16[2,1024,1024]{2,1,0:T(8,128)(2,1)} %bitcast.10, bf16[2,1024,128]{2,1,0:T(8,128)(2,1)} %bitcast.13, s32[1,32]{1,0:T(1,128)} %bitcast.16, bf16[2,1024,128]{2,1,0:T(8,128)(2,1)} %bitcast.14, f32[2,4,1024]{2,1,0:T(4,128)} %bitcast.15, bf16[2,1024,1024]{2,1,0:T(8,128)(2,1)} %bitcast.11), custom_call_target="tpu_custom_call" | custom-call | tf_op jit(solution)/shard_map/pallas_call | solution.py:287
  70.5 2.3 %copy.11 = f32[2,1,1,1024,128]{4,3,2,1,0:T(8,128)} copy(f32[2,1,1,1024,128]{4,3,2,1,0:T(8,128)} %bitcast.12) | data formatting | bytes 2097152

commit v3 on v2

--- a/solution.py
+++ b/solution.py
@@ -97,6 +97,8 @@
     for f in range(f_local):
         mask(f)
         loads[f].wait()
+        if f == 0:
+            pl.semaphore_wait(barrier, count)
         for b in range(blocks):
             part = basis_ref[f, :, b * BLOCK:(b + 1) * BLOCK]
             for low in range(0, n_x * rhs_count, GROUP):
@@ -109,14 +111,9 @@
                         own_ref[f, b] = piece
                     else:
                         sent_ref[k, f, b] = piece.astype(BF16)
-
-    pl.semaphore_wait(barrier, count)
-    for f in range(f_local):
-        for b in range(blocks):
-            for k in range(n_x - 1):
-                copy = sum_copy(f, k, b)
-                copy.start()
-                pending.append((None, copy))
+                        copy = sum_copy(f, k, b)
+                        copy.start()
+                        pending.append((None, copy))
 
     both = jnp.concatenate([coupling_ref[f] for f in range(f_local)], axis=0)
     coupling_t_ref[...] = both.T

time: 74.7 us -> 73 us (0.977)
  Pallas kernels: 69.9 us -> 68.2 us
    pallas_call x1, Pallas kernels: 69.9 us -> 68.2 us  [on_device(): pl.pallas_call(functools.partial(kernel, (n_x, n_y, n_f, entries)), out_s...]
where the time goes in v3:
time: 73 us; the launch traced here: 72.8 us
  Pallas kernels  68.2 us (93%)
  between operations  2.33 us (3%)
  local copies, waits for them, and re-layouts  2.26 us (3%)
    pallas_call x1, Pallas kernels, on_device(): pl.pallas_call(functools.partial(kernel, (n_x, n_y, n_f, entries)), out_s...  68.2 us
    unnamed x1, local copies, waits for them, and re-layouts  2.26 us

profile of v3, /device:TPU:0, one launch (start us, length us, event | category | flops | bytes accessed | tf_op | source)
XLA Modules:
  0.0 72.8 jit_solution(8326561932456810478)
XLA Ops:
  0.6 68.2 %shard_map.77 = (f32[2,1024,128]{2,1,0:T(8,128)}, f32[1,1]{1,0:T(1,128)}) custom-call(bf16[2,1024,1024]{2,1,0:T(8,128)(2,1)} %bitcast.10, bf16[2,1024,128]{2,1,0:T(8,128)(2,1)} %bitcast.13, s32[1,32]{1,0:T(1,128)} %bitcast.16, bf16[2,1024,128]{2,1,0:T(8,128)(2,1)} %bitcast.14, f32[2,4,1024]{2,1,0:T(4,128)} %bitcast.15, bf16[2,1024,1024]{2,1,0:T(8,128)(2,1)} %bitcast.11), custom_call_target="tpu_custom_call" | custom-call | tf_op jit(solution)/shard_map/pallas_call | solution.py:284
  68.9 2.3 %copy.11 = f32[2,1,1,1024,128]{4,3,2,1,0:T(8,128)} copy(f32[2,1,1,1024,128]{4,3,2,1,0:T(8,128)} %bitcast.12) | data formatting | bytes 2097152
